TPU v7x, 32 devices: a whole 2x2x4 slice. The times are simulated.
32 devices in a mesh: gx: 8 (over y, x, core), gy: 4 (over z).
Axes of the slice: x: 2, y: 2, z: 4, core: 2. Of those that a mesh axis runs over, the one named last changes fastest.
Arguments:
- efield_vector: float32 [3, 256, 128, 256], P(None, 'gx', 'gy'), may hold values from -6 to 6
- hfield_vector: float32 [3, 256, 128, 256], P(None, 'gx', 'gy'), may hold values from -6 to 6
- dielectric_grid: float32 [256, 128, 256], P('gx', 'gy'), may hold values from 1 to 6
- sigma_grid: float32 [256, 128, 256], P('gx', 'gy'), may hold values from 0 to 0.5
- substance_label: int32 [256, 128, 256], P('gx', 'gy'), may hold values from 0 to 2
- thermal_state: float32 [1024, 32, 256], P(('gx', 'gy')), may hold values from 0 to 2
- wetness_share: float32 [1024, 32, 256], P(('gx', 'gy')), may hold values from 0.1 to 1
- dielectric_line_choice: int32 [1024, 32, 256], P(('gx', 'gy')), may hold values from 0 to 15
- dielectric_lookup_lines: float32 [4, 16], replicated, may hold values from 0.2 to 2
- dispatch_keeper_map: int32 [32, 32], P(('gx', 'gy')), may hold values from 0 to 31, each once within a row
- arrival_position_map: int32 [32, 32], P(('gx', 'gy')), may hold values from 0 to 31, each once within a row
Outputs:
- final_efield: float32 [3, 256, 128, 256], P(None, 'gx', 'gy')
- final_hfield: float32 [3, 256, 128, 256], P(None, 'gx', 'gy')
- permittivity_out: float32 [256, 128, 256], P('gx', 'gy')
- conductivity_out: float32 [256, 128, 256], P('gx', 'gy')
- temperature_out: float32 [1024, 32, 256], P(('gx', 'gy'))
- moisture_out: float32 [1024, 32, 256], P(('gx', 'gy'))
Inputs may be any that keep to these rules, and one draw needn't show every extreme that they name: Each row names every device index once: block k of device s goes to device dispatch_keeper_map[s, k]. `arrival_position_map`: each row names every slot once.
All inputs are finite; a program needn't handle non-finite values.
Results may differ from a plain program's by a relative error of at most 0.00002.
Values sent between devices are 32-bit elements; how exact they have to be, the bound alone decides.
A program may use at most 128 MiB of HBM per device.

v0:
```python
import jax
import jax.numpy as jnp
from jax import lax
from jax.sharding import PartitionSpec as P

STEPS = 2


TIME_STEP = 0.5
DIFFUSION_FACTOR = 0.2
WARMING_FACTOR = 0.5
BOILING = 1.0
EVAP_RATE = 2.0
VAPOUR_ENTHALPY = 0.8


def passed_along(value, axis, by):
    count = lax.axis_size(axis)
    pairs = [(i, i + by) for i in range(count) if 0 <= i + by < count]
    return lax.ppermute(value, axis, pairs)


def forward_diff(values, border, along):
    extent = values.shape[along]
    nxt = jnp.concatenate(
        [lax.slice_in_dim(values, 1, extent, axis=along), jnp.expand_dims(border, along)],
        axis=along,
    )
    return nxt - values


def backward_diff(values, border, along):
    extent = values.shape[along]
    prev = jnp.concatenate(
        [jnp.expand_dims(border, along), lax.slice_in_dim(values, 0, extent - 1, axis=along)],
        axis=along,
    )
    return values - prev


def lookup(dielectric_lookup_lines, dielectric_line_choice, column):
    moisture_levels = jnp.arange(dielectric_lookup_lines.shape[1], dtype=jnp.int32)
    matches = dielectric_line_choice[None] == moisture_levels[:, None, None, None]
    return jnp.sum(
        jnp.where(matches, dielectric_lookup_lines[column][:, None, None, None], 0.0), axis=0
    )


def thermal_wetness_advance(thermal_state, wetness_share, deposited_wattage, lookup_factors):
    above_depth_entry = jnp.concatenate([thermal_state[..., 1:], thermal_state[..., -1:]], axis=-1)
    beneath_depth_entry = jnp.concatenate(
        [thermal_state[..., :1], thermal_state[..., :-1]], axis=-1
    )
    warmed_voxels = (
        thermal_state
        + DIFFUSION_FACTOR
        * (above_depth_entry - thermal_state + (beneath_depth_entry - thermal_state))
        + WARMING_FACTOR * deposited_wattage
    )
    excess = jnp.maximum(warmed_voxels - BOILING, 0.0)
    vaporised_water = wetness_share * (1.0 - jnp.exp(-EVAP_RATE * excess))
    wetness_refreshed = wetness_share - vaporised_water
    warmth_refreshed = warmed_voxels - VAPOUR_ENTHALPY * vaporised_water
    dielectric_refreshed = 1.0 + lookup_factors[0] + 4.0 * lookup_factors[1] * wetness_refreshed
    sigma_refreshed = 0.1 * lookup_factors[2] + 0.3 * lookup_factors[3] * wetness_refreshed
    return (warmth_refreshed, wetness_refreshed, dielectric_refreshed, sigma_refreshed)


def local(
    efield_vector,
    hfield_vector,
    dielectric_grid,
    sigma_grid,
    substance_label,
    thermal_state,
    wetness_share,
    dielectric_line_choice,
    dielectric_lookup_lines,
    dispatch_keeper_map,
    arrival_position_map,
):
    elec_x, elec_y, elec_z = (efield_vector[0], efield_vector[1], efield_vector[2])
    mag_x, mag_y, mag_z = (hfield_vector[0], hfield_vector[1], hfield_vector[2])
    loss_half = sigma_grid * (0.5 * TIME_STEP) / dielectric_grid
    scale_e = (1.0 - loss_half) / (1.0 + loss_half)
    scale_c = TIME_STEP / dielectric_grid / (1.0 + loss_half)
    zero_z = jnp.zeros_like(elec_x[:, :, 0])
    squares = jnp.zeros_like(dielectric_grid)
    for repeat in range(STEPS):
        border_x = passed_along(jnp.stack([elec_y[0], elec_z[0]]), "gx", -1)
        border_y = passed_along(jnp.stack([elec_x[:, 0], elec_z[:, 0]]), "gy", -1)
        mag_x = mag_x - TIME_STEP * (
            forward_diff(elec_z, border_y[1], 1) - forward_diff(elec_y, zero_z, 2)
        )
        mag_y = mag_y - TIME_STEP * (
            forward_diff(elec_x, zero_z, 2) - forward_diff(elec_z, border_x[1], 0)
        )
        mag_z = mag_z - TIME_STEP * (
            forward_diff(elec_y, border_x[0], 0) - forward_diff(elec_x, border_y[0], 1)
        )
        back_x = passed_along(jnp.stack([mag_y[-1], mag_z[-1]]), "gx", 1)
        back_y = passed_along(jnp.stack([mag_x[:, -1], mag_z[:, -1]]), "gy", 1)
        elec_x = scale_e * elec_x + scale_c * (
            backward_diff(mag_z, back_y[1], 1) - backward_diff(mag_y, zero_z, 2)
        )
        elec_y = scale_e * elec_y + scale_c * (
            backward_diff(mag_x, zero_z, 2) - backward_diff(mag_z, back_x[1], 0)
        )
        elec_z = scale_e * elec_z + scale_c * (
            backward_diff(mag_y, back_x[0], 0) - backward_diff(mag_x, back_y[0], 1)
        )
        squares = squares + (elec_x * elec_x + elec_y * elec_y + elec_z * elec_z)
    deposited_wattage = 0.5 * sigma_grid * squares
    rows_x = lax.axis_size("gx")
    rows_y = lax.axis_size("gy")
    devices = rows_x * rows_y
    depth = deposited_wattage.shape[2]
    width = deposited_wattage.shape[0] * deposited_wattage.shape[1] // devices
    destinations = dispatch_keeper_map[0]
    slots_here = arrival_position_map[0]
    outgoing = deposited_wattage.reshape(devices, width, depth)[jnp.argsort(destinations)]
    arrived = lax.all_to_all(outgoing, ("gx", "gy"), split_axis=0, concat_axis=0, tiled=True)
    wattage_each_tile = arrived[jnp.argsort(slots_here)]
    lookup_factors = [
        lookup(dielectric_lookup_lines, dielectric_line_choice, column) for column in range(4)
    ]
    warmth_refreshed, wetness_refreshed, dielectric_refreshed, sigma_refreshed = (
        thermal_wetness_advance(thermal_state, wetness_share, wattage_each_tile, lookup_factors)
    )
    perm_rows = dielectric_refreshed[slots_here]
    cond_rows = sigma_refreshed[slots_here]
    perm_back, cond_back = (
        lax.all_to_all(perm_rows, ("gx", "gy"), split_axis=0, concat_axis=0, tiled=True),
        lax.all_to_all(cond_rows, ("gx", "gy"), split_axis=0, concat_axis=0, tiled=True),
    )
    perm_cells = perm_back[destinations].reshape(dielectric_grid.shape)
    cond_cells = cond_back[destinations].reshape(sigma_grid.shape)
    product = substance_label == 2
    dielectric_result = jnp.where(product, perm_cells, dielectric_grid)
    sigma_result = jnp.where(product, cond_cells, sigma_grid)
    final_efield = jnp.stack([elec_x, elec_y, elec_z])
    final_hfield = jnp.stack([mag_x, mag_y, mag_z])
    return (
        final_efield,
        final_hfield,
        dielectric_result,
        sigma_result,
        warmth_refreshed,
        wetness_refreshed,
    )


def solution(mesh):
    in_specs = (
        P(None, "gx", "gy", None),
        P(None, "gx", "gy", None),
        P("gx", "gy", None),
        P("gx", "gy", None),
        P("gx", "gy", None),
        P(("gx", "gy"), None, None),
        P(("gx", "gy"), None, None),
        P(("gx", "gy"), None, None),
        P(),
        P(("gx", "gy"), None),
        P(("gx", "gy"), None),
    )
    out_specs = (
        P(None, "gx", "gy", None),
        P(None, "gx", "gy", None),
        P("gx", "gy", None),
        P("gx", "gy", None),
        P(("gx", "gy"), None, None),
        P(("gx", "gy"), None, None),
    )
    return jax.shard_map(local, mesh=mesh, in_specs=in_specs, out_specs=out_specs, check_vma=False)
```

profile of v0, /device:TPU:1, one launch (start us, length us, event | category | flops | bytes accessed | tf_op | source)
XLA Modules:
  0.0 167.8 jit_solution(4948841792476869827)
XLA Ops:
  0.6 2.4 %slice_bitcast_fusion.1 = (f32[32,32,256]{2,1,0:T(8,128)S(1)}, f32[32,32,256]{2,1,0:T(8,128)S(1)}, f32[32,32,256]{2,1,0:T(8,128)S(1)}) fusion(f32[3,32,32,256]{3,2,1,0:T(8,128)} %param.11), kind=kLoop, calls=%fused_computation.78 | loop fusion | bytes 6291456 | tf_op jit(solution)/shard_map/squeeze | solution.py:82
  3.1 1.3 collective-permute-start.1
  4.5 2.0 %collective-permute-start = (f32[2,32,256]{2,1,0:T(8,128)S(1)}, f32[2,32,256]{2,1,0:T(8,128)S(1)}, u32[]{:S(2)}, u32[]{:S(2)}) collective-permute-start(f32[2,32,256]{2,1,0:T(8,128)S(1)} %pad_maximum_fusion.2), channel_id=1, source_target_pairs={{4,0},{8,4},{12,8},{16,12},{20,16},{24,20},{28,24},{5,1},{9,5},{13... | collective-permute-start | bytes 196616 | tf_op jit(solution)/shard_map/ppermute | solution.py:20
  6.5 1.1 slice.313
  7.5 1.3 slice.324
  8.9 1.1 slice.317
  9.9 1.4 slice_bitcast_fusion.3
  11.4 1.3 slice.319
  12.7 1.6 sort.31
  14.3 1.6 sort.32
  16.1 5.2 %fusion.11 = (f32[32,32,256]{2,1,0:T(8,128)S(1)}, f32[32,32,256]{2,1,0:T(8,128)S(1)}, f32[32,32,256]{2,1,0:T(8,128)S(1)}) fusion(f32[1,32,256]{2,1,0:T(8,128)S(1)} %get-tuple-element.58, f32[31,32,256]{2,1,0:T(8,128)} %get-tuple-element.32, f32[32,32,255]{2,1,0:T(8,128)} %slice.324, f32[3,32,32,256]{3,2,1,0:T(8,128)} %param.12, ...), kind=kLoop, calls=%fused_computation.29 | loop fusion | flops 4980736 | bytes 15720448 | tf_op jit(solution)/shard_map/sub | solution.py:95
  21.7 5.4 %collective-permute-start.2 = (f32[2,32,256]{2,0,1:T(2,128)S(1)}, f32[2,32,256]{2,0,1:T(2,128)S(1)}, u32[]{:S(2)}, u32[]{:S(2)}) collective-permute-start(f32[2,32,256]{2,0,1:T(2,128)S(1)} %pad_maximum_fusion.4), channel_id=1, source_target_pairs={{0,1},{1,2},{2,3},{4,5},{5,6},{6,7},{8,9},{9,10},{10,11},{12,13},{... | collective-permute-start | bytes 196616 | tf_op jit(solution)/shard_map/ppermute | solution.py:20
  27.1 3.7 %collective-permute-start.3 = (f32[2,32,256]{2,1,0:T(8,128)S(1)}, f32[2,32,256]{2,1,0:T(8,128)S(1)}, u32[]{:S(2)}, u32[]{:S(2)}) collective-permute-start(f32[2,32,256]{2,1,0:T(8,128)S(1)} %pad_maximum_fusion.5), channel_id=1, source_target_pairs={{0,4},{4,8},{8,12},{12,16},{16,20},{20,24},{24,28},{1,5},{5,9},{9,... | collective-permute-start | bytes 196616 | tf_op jit(solution)/shard_map/ppermute | solution.py:20
  30.9 1.1 fusion.8
  32.2 1.5 fusion.14
  34.9 1.9 %collective-permute-start.4 = (f32[2,32,256]{2,1,0:T(8,128)S(1)}, f32[2,32,256]{2,1,0:T(8,128)S(1)}, u32[]{:S(2)}, u32[]{:S(2)}) collective-permute-start(f32[2,32,256]{2,1,0:T(8,128)S(1)} %pad_maximum_fusion.6), channel_id=1, source_target_pairs={{4,0},{8,4},{12,8},{16,12},{20,16},{24,20},{28,24},{5,1},{9,5},{13... | collective-permute-start | bytes 196616 | tf_op jit(solution)/shard_map/ppermute | solution.py:20
  36.9 1.3 collective-permute-start.5
  38.2 2.9 %collective-permute-done.4 = f32[2,32,256]{2,1,0:T(8,128)S(1)} collective-permute-done((f32[2,32,256]{2,1,0:T(8,128)S(1)}, f32[2,32,256]{2,1,0:T(8,128)S(1)}, u32[]{:S(2)}, u32[]{:S(2)}) %collective-permute-start.4) | collective-permute-done | bytes 65568 | tf_op jit(solution)/shard_map/ppermute | solution.py:20
  41.1 0.8 collective-permute-done.5
  42.0 1.9 %fusion.23 = (f32[32,32,256]{2,1,0:T(8,128)S(1)}, f32[32,32,256]{2,1,0:T(8,128)S(1)}, f32[32,32,256]{2,1,0:T(8,128)S(1)}) fusion(f32[32,32,256]{2,1,0:T(8,128)S(1)} %get-tuple-element.31, f32[32,32,256]{2,1,0:T(8,128)S(1)} %get-tuple-element.28, f32[32,1,256]{2,1,0:T(1,128)S(1)} %get-tuple-element.50, f32[32,31,256]{2,1,0:T(8,128)S(1)} %slice.344, ...), kind=kLoop, calls=%fused_computation.47 | loop fusion | flops 4980736 | bytes 15720448 | tf_op jit(solution)/shard_map/sub | solution.py:92
  44.1 5.6 %collective-permute-start.7 = (f32[2,32,256]{2,1,0:T(8,128)S(1)}, f32[2,32,256]{2,1,0:T(8,128)S(1)}, u32[]{:S(2)}, u32[]{:S(2)}) collective-permute-start(f32[2,32,256]{2,1,0:T(8,128)S(1)} %pad_maximum_fusion.9), channel_id=1, source_target_pairs={{0,4},{4,8},{8,12},{12,16},{16,20},{20,24},{24,28},{1,5},{5,9},{9,... | collective-permute-start | bytes 196616 | tf_op jit(solution)/shard_map/ppermute | solution.py:20
  49.9 3.2 %collective-permute-start.6 = (f32[2,32,256]{2,0,1:T(2,128)S(1)}, f32[2,32,256]{2,0,1:T(2,128)S(1)}, u32[]{:S(2)}, u32[]{:S(2)}) collective-permute-start(f32[2,32,256]{2,0,1:T(2,128)S(1)} %pad_maximum_fusion.8), channel_id=1, source_target_pairs={{0,1},{1,2},{2,3},{4,5},{5,6},{6,7},{8,9},{9,10},{10,11},{12,13},{... | collective-permute-start | bytes 196616 | tf_op jit(solution)/shard_map/ppermute | solution.py:20
  53.1 1.3 collective-permute-done.6
  54.5 3.6 %add_multiply_fusion = (f32[32,32,256]{2,1,0:T(8,128)}, f32[32,32,256]{2,1,0:T(8,128)}, f32[32,32,256]{2,1,0:T(8,128)}, f32[32,32,256]{2,1,0:T(8,128)}) fusion(f32[32,32,256]{2,1,0:T(8,128)S(1)} %get-tuple-element.28, f32[32,32,256]{2,1,0:T(8,128)S(1)} %get-tuple-element.27, f32[32,32,256]{2,1,0:T(8,128)S(1)} %get-tuple-element.24, ...), kind=kLoop, calls=%fused_computation.76 | loop fusion | flops 9175040 | bytes 19914752 | tf_op jit(solution)/shard_map/mul | solution.py:113
  58.1 2.8 %gather_fusion = f32[32,32,256]{2,1,0:T(8,128)} fusion(f32[32,32,256]{2,1,0:T(8,128)} %get-tuple-element.20, s32[1024]{0:T(1024)S(1)} %pad_clamp_fusion.3), kind=kCustom, calls=%fused_computation | custom fusion | bytes 2097280 | tf_op jit(solution)/shard_map/gather | solution.py:121
  60.9 5.8 %all-to-all-start = ((f32[32,32,256]{2,1,0:T(8,128)}), f32[32,32,256]{2,1,0:T(8,128)}, u32[]{:S(2)}, u32[]{:S(2)}) async-start(f32[32,32,256]{2,1,0:T(8,128)} %gather_fusion), calls=%async_computation | async-start | bytes 2097152 | tf_op jit(solution)/shard_map/all_to_all | solution.py:122
  66.7 2.5 %fusion.50 = (f32[32,32,1]{2,1,0:T(8,128)}, f32[32,32,1]{2,1,0:T(8,128)}) fusion(f32[32,32,256]{2,1,0:T(8,128)} %param.16), kind=kLoop, calls=%fused_computation.128 | loop fusion | bytes 16384 | tf_op jit(solution)/shard_map/slice | solution.py:50
  69.3 1.7 %fusion.49 = (f32[32,32,255]{2,1,0:T(8,128)}, f32[32,32,255]{2,1,0:T(8,128)}) fusion(f32[32,32,256]{2,1,0:T(8,128)S(1)} %copy-done.1), kind=kLoop, calls=%fused_computation.127 | loop fusion | bytes 4177920 | tf_op jit(solution)/shard_map/slice | solution.py:50
  71.0 9.0 %select_reduce_fusion.1 = (f32[32,32,256]{2,1,0:T(8,128)}, f32[32,32,256]{2,1,0:T(8,128)}, f32[32,32,256]{2,1,0:T(8,128)}, f32[32,32,256]{2,1,0:T(8,128)}) fusion(f32[16]{0:T(128)S(1)} %get-tuple-element.65, s32[32,32,256]{2,1,0:T(8,128)S(1)} %copy-done.12, f32[16]{0:T(128)S(1)} %get-tuple-element.64, f32[16]{0:T(128)S(1)} %get-tuple-element.63, ...), kind=kLoop, calls=%fused_computation.7 | loop fusion | flops 36700160 | bytes 5243136 | tf_op jit(solution)/shard_map/reduce_sum | solution.py:44
  80.0 13.1 %all-to-all-done = f32[32,32,256]{2,1,0:T(8,128)} async-done(((f32[32,32,256]{2,1,0:T(8,128)}), f32[32,32,256]{2,1,0:T(8,128)}, u32[]{:S(2)}, u32[]{:S(2)}) %all-to-all-start) | async-done | bytes 1048608 | tf_op jit(solution)/shard_map/all_to_all | solution.py:122
  93.1 2.8 %gather_fusion.1 = f32[32,32,256]{2,1,0:T(8,128)} fusion(f32[32,32,256]{2,1,0:T(8,128)} %all-to-all-done, s32[1024]{0:T(1024)S(1)} %pad_clamp_fusion.2), kind=kCustom, calls=%fused_computation.1 | custom fusion | bytes 2097280 | tf_op jit(solution)/shard_map/gather | solution.py:123
  95.9 4.8 %multiply_subtract_fusion = (f32[32,32,256]{2,1,0:T(8,128)}, f32[32,32,256]{2,1,0:T(8,128)S(1)}) fusion(f32[32,32,256]{2,1,0:T(8,128)} %param.17, f32[32,32,256]{2,1,0:T(8,128)} %gather_fusion.1, f32[32,32,256]{2,1,0:T(8,128)} %param.16, f32[32,32,255]{2,1,0:T(8,128)} %get-tuple-element.40, f32[32,32,1]{2,1,0:T(8,128)} %get-tuple-element.42, ...), kind=kLoop, calls=%fused_computation.71 | loop fusion | flops 4194304 | bytes 7340032 | tf_op jit(solution)/shard_map/sub | solution.py:63
  100.7 2.0 %multiply_add_fusion = (f32[32,32,256]{2,1,0:T(8,128)}, f32[32,32,256]{2,1,0:T(8,128)}) fusion(f32[32,32,256]{2,1,0:T(8,128)S(1)} %copy-done.10, f32[32,32,256]{2,1,0:T(8,128)S(1)} %copy-done.9, f32[32,32,256]{2,1,0:T(8,128)S(1)} %copy-done.11, f32[32,32,256]{2,1,0:T(8,128)S(1)} %get-tuple-element.15), kind=kLoop, calls=%fused_computation.72 | loop fusion | flops 2621440 | bytes 6291456 | tf_op jit(solution)/shard_map/add | solution.py:65
  102.7 2.8 %gather_fusion.4 = f32[32,32,256]{2,1,0:T(8,128)} fusion(f32[32,32,256]{2,1,0:T(8,128)} %get-tuple-element.18, s32[1024]{0:T(1024)S(1)} %pad_clamp_fusion.1), kind=kCustom, calls=%fused_computation.4 | custom fusion | bytes 2097280 | tf_op jit(solution)/shard_map/gather | solution.py:131
  105.5 3.2 %all-to-all-start.2 = ((f32[32,32,256]{2,1,0:T(8,128)}), f32[32,32,256]{2,1,0:T(8,128)}, u32[]{:S(2)}, u32[]{:S(2)}) async-start(f32[32,32,256]{2,1,0:T(8,128)} %gather_fusion.4), calls=%async_computation.2 | async-start | bytes 2097152 | tf_op jit(solution)/shard_map/all_to_all | solution.py:134
  108.7 3.2 %multiply_add_fusion.1 = f32[32,32,256]{2,1,0:T(8,128)} fusion(f32[32,32,256]{2,1,0:T(8,128)} %get-tuple-element.19, f32[32,32,256]{2,1,0:T(8,128)} %get-tuple-element.12, f32[32,32,256]{2,1,0:T(8,128)} %get-tuple-element.13), kind=kLoop, calls=%fused_computation.73 | loop fusion | flops 1048576 | bytes 4194304 | tf_op jit(solution)/shard_map/add | solution.py:64
  112.0 2.8 %gather_fusion.2 = f32[32,32,256]{2,1,0:T(8,128)} fusion(f32[32,32,256]{2,1,0:T(8,128)} %multiply_add_fusion.1, s32[1024]{0:T(1024)S(1)} %pad_clamp_fusion.1), kind=kCustom, calls=%fused_computation.2 | custom fusion | bytes 2097280 | tf_op jit(solution)/shard_map/gather | solution.py:130
  114.8 20.4 %all-to-all-done.2 = f32[32,32,256]{2,1,0:T(8,128)} async-done(((f32[32,32,256]{2,1,0:T(8,128)}), f32[32,32,256]{2,1,0:T(8,128)}, u32[]{:S(2)}, u32[]{:S(2)}) %all-to-all-start.2) | async-done | bytes 1048608 | tf_op jit(solution)/shard_map/all_to_all | solution.py:134
  135.1 3.2 %all-to-all-start.1 = ((f32[32,32,256]{2,1,0:T(8,128)}), f32[32,32,256]{2,1,0:T(8,128)}, u32[]{:S(2)}, u32[]{:S(2)}) async-start(f32[32,32,256]{2,1,0:T(8,128)} %gather_fusion.2), calls=%async_computation.1 | async-start | bytes 2097152 | tf_op jit(solution)/shard_map/all_to_all | solution.py:133
  138.4 1.9 %pad_maximum_fusion.1 = f32[3,32,32,256]{3,2,1,0:T(8,128)} fusion(f32[1,32,32,256]{3,2,1,0:T(8,128)S(1)} %bitcast.108, f32[1,32,32,256]{3,2,1,0:T(8,128)S(1)} %bitcast.112, f32[1,32,32,256]{3,2,1,0:T(8,128)S(1)} %bitcast.106), kind=kLoop, calls=%fused_computation.12 | loop fusion | flops 1572864 | bytes 6291456 | tf_op jit(solution)/shard_map/stack | solution.py:142
  140.3 0.5 copy-done.7
  140.8 0.6 copy-done.8
  141.4 2.0 %pad_maximum_fusion = f32[3,32,32,256]{3,2,1,0:T(8,128)} fusion(f32[1,32,32,256]{3,2,1,0:T(8,128)S(1)} %bitcast.115, f32[1,32,32,256]{3,2,1,0:T(8,128)S(1)} %bitcast.114, f32[1,32,32,256]{3,2,1,0:T(8,128)S(1)} %bitcast.113), kind=kLoop, calls=%fused_computation.11 | loop fusion | flops 1572864 | bytes 6291456 | tf_op jit(solution)/shard_map/stack | solution.py:141
  143.4 1.8 %gather_fusion.5 = f32[32,32,256]{2,1,0:T(8,128)S(1)} fusion(f32[32,32,256]{2,1,0:T(8,128)} %all-to-all-done.2, s32[1024]{0:T(1024)S(1)} %pad_clamp_fusion), kind=kCustom, calls=%fused_computation.5 | custom fusion | bytes 2097280 | tf_op jit(solution)/shard_map/gather | solution.py:137
  145.3 2.6 %fusion.44 = (f32[32,32,256]{2,1,0:T(8,128)}, pred[32,32,256]{2,1,0:T(8,128)(4,1)S(1)}) fusion(f32[32,32,256]{2,1,0:T(8,128)S(1)} %gather_fusion.5, f32[32,32,256]{2,1,0:T(8,128)S(1)} %copy-done.3, s32[32,32,256]{2,1,0:T(8,128)} %param.15), kind=kLoop, calls=%fused_computation.126 | loop fusion | flops 524288 | bytes 4456448 | tf_op jit(solution)/shard_map/jit(_where)/select_n | solution.py:140
  147.9 16.9 %all-to-all-done.1 = f32[32,32,256]{2,1,0:T(8,128)} async-done(((f32[32,32,256]{2,1,0:T(8,128)}), f32[32,32,256]{2,1,0:T(8,128)}, u32[]{:S(2)}, u32[]{:S(2)}) %all-to-all-start.1) | async-done | bytes 1048608 | tf_op jit(solution)/shard_map/all_to_all | solution.py:133
  164.8 1.8 %gather_fusion.3 = f32[32,32,256]{2,1,0:T(8,128)S(1)} fusion(f32[32,32,256]{2,1,0:T(8,128)} %all-to-all-done.1, s32[1024]{0:T(1024)S(1)} %pad_clamp_fusion), kind=kCustom, calls=%fused_computation.3 | custom fusion | bytes 2097280 | tf_op jit(solution)/shard_map/gather | solution.py:136
  166.6 1.2 select_n.54
  (86 shorter events, 2.5 us)
Async XLA Ops:
  0.6 3.8 %copy-start = (f32[3,32,32,256]{3,2,1,0:T(8,128)S(1)}, f32[3,32,32,256]{3,2,1,0:T(8,128)}, u32[]{:S(2)}) copy-start(f32[3,32,32,256]{3,2,1,0:T(8,128)} %param.11) | copy-start | bytes 9437188
  3.1 12.8 %collective-permute-start.1 = (f32[2,32,256]{2,0,1:T(2,128)S(1)}, f32[2,32,256]{2,0,1:T(2,128)S(1)}, u32[]{:S(2)}, u32[]{:S(2)}) collective-permute-start(f32[2,32,256]{2,0,1:T(2,128)S(1)} %pad_maximum_fusion.3), channel_id=1, source_target_pairs={{1,0},{2,1},{3,2},{5,4},{6,5},{7,6},{9,8},{10,9},{11,10},{13,12},{... | collective-permute-start | bytes 196616 | tf_op jit(solution)/shard_map/ppermute | solution.py:20
  4.5 11.6 %collective-permute-start = (f32[2,32,256]{2,1,0:T(8,128)S(1)}, f32[2,32,256]{2,1,0:T(8,128)S(1)}, u32[]{:S(2)}, u32[]{:S(2)}) collective-permute-start(f32[2,32,256]{2,1,0:T(8,128)S(1)} %pad_maximum_fusion.2), channel_id=1, source_target_pairs={{4,0},{8,4},{12,8},{16,12},{20,16},{24,20},{28,24},{5,1},{9,5},{13... | collective-permute-start | bytes 196616 | tf_op jit(solution)/shard_map/ppermute | solution.py:20
  9.9 2.7 %copy-start.15 = (s32[1,32]{1,0:T(1,128)S(1)}, s32[1,32]{1,0:T(1,128)}, u32[]{:S(2)}) copy-start(s32[1,32]{1,0:T(1,128)} %param.20) | copy-start | bytes 388
  9.9 4.4 %copy-start.14 = (s32[1,32]{1,0:T(1,128)S(1)}, s32[1,32]{1,0:T(1,128)}, u32[]{:S(2)}) copy-start(s32[1,32]{1,0:T(1,128)} %param.21) | copy-start | bytes 388
  9.9 6.0 %copy-start.13 = (f32[4,16]{1,0:T(4,128)S(1)}, f32[4,16]{1,0:T(4,128)}, u32[]{:S(2)}) copy-start(f32[4,16]{1,0:T(4,128)} %param.19) | copy-start | bytes 772
  21.3 9.6 %copy-start.2 = (f32[32,32,256]{2,1,0:T(8,128)S(1)}, f32[32,32,256]{2,1,0:T(8,128)}, u32[]{:S(2)}) copy-start(f32[32,32,256]{2,1,0:T(8,128)} %param.14) | copy-start | bytes 3145732
  21.3 9.6 %copy-start.4 = (f32[32,32,256]{2,1,0:T(8,128)S(1)}, f32[32,32,256]{2,1,0:T(8,128)}, u32[]{:S(2)}) copy-start(f32[32,32,256]{2,1,0:T(8,128)} %param.13) | copy-start | bytes 3145732
  21.7 9.2 %collective-permute-start.2 = (f32[2,32,256]{2,0,1:T(2,128)S(1)}, f32[2,32,256]{2,0,1:T(2,128)S(1)}, u32[]{:S(2)}, u32[]{:S(2)}) collective-permute-start(f32[2,32,256]{2,0,1:T(2,128)S(1)} %pad_maximum_fusion.4), channel_id=1, source_target_pairs={{0,1},{1,2},{2,3},{4,5},{5,6},{6,7},{8,9},{9,10},{10,11},{12,13},{... | collective-permute-start | bytes 196616 | tf_op jit(solution)/shard_map/ppermute | solution.py:20
  27.1 5.1 %collective-permute-start.3 = (f32[2,32,256]{2,1,0:T(8,128)S(1)}, f32[2,32,256]{2,1,0:T(8,128)S(1)}, u32[]{:S(2)}, u32[]{:S(2)}) collective-permute-start(f32[2,32,256]{2,1,0:T(8,128)S(1)} %pad_maximum_fusion.5), channel_id=1, source_target_pairs={{0,4},{4,8},{8,12},{12,16},{16,20},{20,24},{24,28},{1,5},{5,9},{9,... | collective-permute-start | bytes 196616 | tf_op jit(solution)/shard_map/ppermute | solution.py:20
  34.9 6.2 %collective-permute-start.4 = (f32[2,32,256]{2,1,0:T(8,128)S(1)}, f32[2,32,256]{2,1,0:T(8,128)S(1)}, u32[]{:S(2)}, u32[]{:S(2)}) collective-permute-start(f32[2,32,256]{2,1,0:T(8,128)S(1)} %pad_maximum_fusion.6), channel_id=1, source_target_pairs={{4,0},{8,4},{12,8},{16,12},{20,16},{24,20},{28,24},{5,1},{9,5},{13... | collective-permute-start | bytes 196616 | tf_op jit(solution)/shard_map/ppermute | solution.py:20
  36.9 5.0 %collective-permute-start.5 = (f32[2,32,256]{2,0,1:T(2,128)S(1)}, f32[2,32,256]{2,0,1:T(2,128)S(1)}, u32[]{:S(2)}, u32[]{:S(2)}) collective-permute-start(f32[2,32,256]{2,0,1:T(2,128)S(1)} %pad_maximum_fusion.7), channel_id=1, source_target_pairs={{1,0},{2,1},{3,2},{5,4},{6,5},{7,6},{9,8},{10,9},{11,10},{13,12},{... | collective-permute-start | bytes 196616 | tf_op jit(solution)/shard_map/ppermute | solution.py:20
  44.1 9.0 %collective-permute-start.7 = (f32[2,32,256]{2,1,0:T(8,128)S(1)}, f32[2,32,256]{2,1,0:T(8,128)S(1)}, u32[]{:S(2)}, u32[]{:S(2)}) collective-permute-start(f32[2,32,256]{2,1,0:T(8,128)S(1)} %pad_maximum_fusion.9), channel_id=1, source_target_pairs={{0,4},{4,8},{8,12},{12,16},{16,20},{20,24},{24,28},{1,5},{5,9},{9,... | collective-permute-start | bytes 196616 | tf_op jit(solution)/shard_map/ppermute | solution.py:20
  49.9 4.5 %collective-permute-start.6 = (f32[2,32,256]{2,0,1:T(2,128)S(1)}, f32[2,32,256]{2,0,1:T(2,128)S(1)}, u32[]{:S(2)}, u32[]{:S(2)}) collective-permute-start(f32[2,32,256]{2,0,1:T(2,128)S(1)} %pad_maximum_fusion.8), channel_id=1, source_target_pairs={{0,1},{1,2},{2,3},{4,5},{5,6},{6,7},{8,9},{9,10},{10,11},{12,13},{... | collective-permute-start | bytes 196616 | tf_op jit(solution)/shard_map/ppermute | solution.py:20
  60.9 32.2 %all-to-all-start = ((f32[32,32,256]{2,1,0:T(8,128)}), f32[32,32,256]{2,1,0:T(8,128)}, u32[]{:S(2)}, u32[]{:S(2)}) async-start(f32[32,32,256]{2,1,0:T(8,128)} %gather_fusion), calls=%async_computation | async-start | bytes 2097152 | tf_op jit(solution)/shard_map/all_to_all | solution.py:122
  66.7 2.5 %copy-start.1 = (f32[32,32,256]{2,1,0:T(8,128)S(1)}, f32[32,32,256]{2,1,0:T(8,128)}, u32[]{:S(2)}) copy-start(f32[32,32,256]{2,1,0:T(8,128)} %param.16) | copy-start | bytes 3145732
  66.7 4.3 %copy-start.12 = (s32[32,32,256]{2,1,0:T(8,128)S(1)}, s32[32,32,256]{2,1,0:T(8,128)}, u32[]{:S(2)}) copy-start(s32[32,32,256]{2,1,0:T(8,128)} %param.18) | copy-start | bytes 3145732
  95.9 4.8 %copy-start.9 = (f32[32,32,256]{2,1,0:T(8,128)S(1)}, f32[32,32,256]{2,1,0:T(8,128)}, u32[]{:S(2)}) copy-start(f32[32,32,256]{2,1,0:T(8,128)} %get-tuple-element.10) | copy-start | bytes 3145732
  95.9 4.8 %copy-start.10 = (f32[32,32,256]{2,1,0:T(8,128)S(1)}, f32[32,32,256]{2,1,0:T(8,128)}, u32[]{:S(2)}) copy-start(f32[32,32,256]{2,1,0:T(8,128)} %get-tuple-element.11) | copy-start | bytes 3145732
  95.9 4.8 %copy-start.11 = (f32[32,32,256]{2,1,0:T(8,128)S(1)}, f32[32,32,256]{2,1,0:T(8,128)}, u32[]{:S(2)}) copy-start(f32[32,32,256]{2,1,0:T(8,128)} %param.17) | copy-start | bytes 3145732
  105.5 29.6 %all-to-all-start.2 = ((f32[32,32,256]{2,1,0:T(8,128)}), f32[32,32,256]{2,1,0:T(8,128)}, u32[]{:S(2)}, u32[]{:S(2)}) async-start(f32[32,32,256]{2,1,0:T(8,128)} %gather_fusion.4), calls=%async_computation.2 | async-start | bytes 2097152 | tf_op jit(solution)/shard_map/all_to_all | solution.py:134
  135.1 29.6 %all-to-all-start.1 = ((f32[32,32,256]{2,1,0:T(8,128)}), f32[32,32,256]{2,1,0:T(8,128)}, u32[]{:S(2)}, u32[]{:S(2)}) async-start(f32[32,32,256]{2,1,0:T(8,128)} %gather_fusion.2), calls=%async_computation.1 | async-start | bytes 2097152 | tf_op jit(solution)/shard_map/all_to_all | solution.py:133
  138.4 1.9 %copy-start.6 = (f32[32,32,256]{2,1,0:T(8,128)S(1)}, f32[32,32,256]{2,1,0:T(8,128)}, u32[]{:S(2)}) copy-start(f32[32,32,256]{2,1,0:T(8,128)} %get-tuple-element.21) | copy-start | bytes 3145732
  138.4 2.4 %copy-start.7 = (f32[32,32,256]{2,1,0:T(8,128)S(1)}, f32[32,32,256]{2,1,0:T(8,128)}, u32[]{:S(2)}) copy-start(f32[32,32,256]{2,1,0:T(8,128)} %get-tuple-element.22) | copy-start | bytes 3145732
  138.4 3.0 %copy-start.8 = (f32[32,32,256]{2,1,0:T(8,128)S(1)}, f32[32,32,256]{2,1,0:T(8,128)}, u32[]{:S(2)}) copy-start(f32[32,32,256]{2,1,0:T(8,128)} %get-tuple-element.23) | copy-start | bytes 3145732
  141.4 3.9 %copy-start.3 = (f32[32,32,256]{2,1,0:T(8,128)S(1)}, f32[32,32,256]{2,1,0:T(8,128)}, u32[]{:S(2)}) copy-start(f32[32,32,256]{2,1,0:T(8,128)} %param.14) | copy-start | bytes 3145732
  145.3 21.3 %copy-start.5 = (f32[32,32,256]{2,1,0:T(8,128)S(1)}, f32[32,32,256]{2,1,0:T(8,128)}, u32[]{:S(2)}) copy-start(f32[32,32,256]{2,1,0:T(8,128)} %param.13) | copy-start | bytes 3145732
where the time goes:
time: 169 us; the launch traced here: 168 us
  waiting for transfers between devices  55.6 us (33%)
  other arithmetic  43.5 us (26%)
  starting transfers between devices  36.7 us (22%)
  local copies, waits for them, and re-layouts  30.8 us (18%)
    ppermute x8, starting transfers between devices, passed_along(): return lax.ppermute(value, axis, pairs)  24.5 us
    all_to_all x1, waiting for transfers between devices, local(): lax.all_to_all(cond_rows, ('gx', 'gy'), split_axis=0, concat_axis=0, tile...  20.4 us
    all_to_all x1, waiting for transfers between devices, local(): lax.all_to_all(perm_rows, ('gx', 'gy'), split_axis=0, concat_axis=0, tile...  16.9 us
    all_to_all x1, waiting for transfers between devices, local(): lax.all_to_all(outgoing, ('gx', 'gy'), split_axis=0, concat_axis=0, tiled...  13.1 us
    reduce_sum x1, other arithmetic, lookup(): jnp.sum(jnp.where(matches, dielectric_lookup_lines[column][:, None, None,...  8.97 us
    slice x11, local copies, waits for them, and re-layouts, forward_diff(): lax.slice_in_dim(values, 1, extent, axis=along)  7.32 us
    all_to_all x1, starting transfers between devices, local(): lax.all_to_all(outgoing, ('gx', 'gy'), split_axis=0, concat_axis=0, tiled...  5.77 us
    sub x1, other arithmetic, local(): mag_y - TIME_STEP * (forward_diff(elec_x, zero_z, 2) - forward_diff(elec_...  5.23 us
  transfers between devices with their start and end apart: 11, of which 7 were waited for; matrix products, arithmetic and copies ran while one was open for 23% of the time, Pallas kernels for 0%

commit v1 on v0

v1 whole, which is shorter than its diff:
```python
import functools

import jax
import jax.numpy as jnp
from jax import lax
from jax.experimental import pallas as pl
from jax.experimental.pallas import tpu as pltpu
from jax.sharding import PartitionSpec as P

STEPS = 2
TIME_STEP = 0.5
DIFFUSION_FACTOR = 0.2
WARMING_FACTOR = 0.5
BOILING = 1.0
EVAP_RATE = 2.0
VAPOUR_ENTHALPY = 0.8
MESH = pl.DeviceIdType.MESH


def kernel(
    nx, ny, maps, table,
    e_in, h_in, eps_in, sig_in, lab_in, t_in, w_in, c_in,
    e_out, h_out, perm_out, cond_out, temp_out, moist_out,
    e, h, eps, sig, lab, temp, wet, choice,
    scale_e, scale_c, squares, power,
    send_c, recv_c, send_p, recv_p, tmp_t, tmp_m, recv_m,
    new_perm, new_cond, temp_stage, moist_stage, perm_stage, cond_stage,
    send_y, halo_x, halo_y,
    in_sem, out_sem, hx_send, hx_recv, hy_send, hy_recv,
    sc_sem, rc_sem, sp_sem, rp_sem, sm_sem, rm_sem,
):
    n = nx * ny
    i = lax.axis_index("gx")
    j = lax.axis_index("gy")
    me = i * ny + j
    _, cx, cy, depth = e.shape
    width = cy * cx // n
    per_plane = cy // width

    loads = [
        pltpu.make_async_copy(src, dst, in_sem.at[q])
        for q, (src, dst) in enumerate([
            (e_in, e), (c_in, choice), (eps_in, eps), (sig_in, sig), (h_in, h),
            (t_in, temp), (w_in, wet), (lab_in, lab),
        ])
    ]
    for load in loads:
        load.start()

    def device_of(s):
        return (s // ny, lax.rem(s, ny))

    barrier = pltpu.get_barrier_semaphore()

    def greet(d, _):
        pl.semaphore_signal(
            barrier, inc=1, device_id=device_of(lax.rem(me + d, n)), device_id_type=MESH
        )
        return 0

    lax.fori_loop(1, n, greet, 0)

    for exchange in range(2 * STEPS):
        forward = exchange % 2 == 0

        @pl.when(i == (nx - 1 if forward else 0))
        def _():
            halo_x[exchange] = jnp.zeros_like(halo_x[exchange])

        @pl.when(j == (ny - 1 if forward else 0))
        def _():
            halo_y[exchange] = jnp.zeros_like(halo_y[exchange])

    def plane_of(ref, x):
        return ref[pl.ds(x * per_plane, per_plane)].reshape(cy, depth)

    def set_plane(ref, x, value):
        ref[pl.ds(x * per_plane, per_plane)] = value.reshape(per_plane, width, depth)

    def halo_copies(exchange):
        forward = exchange % 2 == 0
        if forward:
            source, by = e.at[pl.ds(1, 2), 0], -1
        else:
            source, by = h.at[pl.ds(1, 2), cx - 1], 1
        x_copy = pltpu.make_async_remote_copy(
            src_ref=source, dst_ref=halo_x.at[exchange],
            send_sem=hx_send.at[exchange], recv_sem=hx_recv.at[exchange],
            device_id=(lax.rem(i + by + nx, nx), j), device_id_type=MESH,
        )
        y_copy = pltpu.make_async_remote_copy(
            src_ref=send_y.at[exchange], dst_ref=halo_y.at[exchange],
            send_sem=hy_send.at[exchange], recv_sem=hy_recv.at[exchange],
            device_id=(i, lax.rem(j + by + ny, ny)), device_id_type=MESH,
        )
        first_x, last_x = i > 0, i < nx - 1
        first_y, last_y = j > 0, j < ny - 1
        if forward:
            return x_copy, y_copy, first_x, first_y, last_x, last_y
        return x_copy, y_copy, last_x, last_y, first_x, first_y

    def start_halo(exchange):
        x_copy, y_copy, sends_x, sends_y, _, _ = halo_copies(exchange)
        pl.when(sends_y)(y_copy.start)
        pl.when(sends_x)(x_copy.start)

    def await_halo(exchange):
        x_copy, y_copy, sends_x, sends_y, gets_x, gets_y = halo_copies(exchange)
        pl.when(gets_y)(y_copy.wait_recv)
        pl.when(gets_x)(x_copy.wait_recv)
        pl.when(sends_y)(y_copy.wait_send)
        pl.when(sends_x)(x_copy.wait_send)

    def block_copy(source, landing, send_sem, recv_sem, partner, slot):
        return pltpu.make_async_remote_copy(
            src_ref=source.at[partner], dst_ref=landing.at[slot],
            send_sem=send_sem.at[partner], recv_sem=recv_sem.at[slot],
            device_id=device_of(partner), device_id_type=MESH,
        )

    def send_choice(d, _):
        t = lax.rem(me + d, n)
        send_c[t] = choice[maps[1, t]].astype(jnp.float32)
        block_copy(send_c, recv_c, sc_sem, rc_sem, t, me).start()
        return 0

    cuts = [1 + (n - 1) * q // 4 for q in range(5)]

    row = lax.broadcasted_iota(jnp.int32, (cy, depth), 0)
    lane = lax.broadcasted_iota(jnp.int32, (cy, depth), 1)

    def next_y(v, border):
        return jnp.where(row == cy - 1, border, pltpu.roll(v, cy - 1, 0))

    def prev_y(v, border):
        return jnp.where(row == 0, border, pltpu.roll(v, 1, 0))

    def next_z(v):
        return jnp.where(lane == depth - 1, 0.0, pltpu.roll(v, depth - 1, 1))

    def prev_z(v):
        return jnp.where(lane == 0, 0.0, pltpu.roll(v, 1, 1))

    def h_plane(step, x, ey_next, ez_next):
        ex, ey, ez = e[0, x], e[1, x], e[2, x]
        ex_up = next_y(ex, halo_y[2 * step, 0, x])
        ez_up = next_y(ez, halo_y[2 * step, 1, x])
        hx = h[0, x] - TIME_STEP * ((ez_up - ez) - (next_z(ey) - ey))
        hy = h[1, x] - TIME_STEP * ((next_z(ex) - ex) - (ez_next - ez))
        hz = h[2, x] - TIME_STEP * ((ey_next - ey) - (ex_up - ex))
        h[0, x] = hx
        h[1, x] = hy
        h[2, x] = hz
        send_y[2 * step + 1, 0, x] = hx[cy - 1:, :]
        send_y[2 * step + 1, 1, x] = hz[cy - 1:, :]

    def e_plane(step, x, hy_prev, hz_prev):
        hx, hy, hz = h[0, x], h[1, x], h[2, x]
        se, sc = plane_of(scale_e, x), plane_of(scale_c, x)
        hx_low = prev_y(hx, halo_y[2 * step + 1, 0, x])
        hz_low = prev_y(hz, halo_y[2 * step + 1, 1, x])
        ex = se * e[0, x] + sc * ((hz - hz_low) - (hy - prev_z(hy)))
        ey = se * e[1, x] + sc * ((hx - prev_z(hx)) - (hz - hz_prev))
        ez = se * e[2, x] + sc * ((hy - hy_prev) - (hx - hx_low))
        e[0, x] = ex
        e[1, x] = ey
        e[2, x] = ez
        added = ex * ex + ey * ey + ez * ez
        if step > 0:
            added = plane_of(squares, x) + added
        if step < STEPS - 1:
            set_plane(squares, x, added)
            send_y[2 * step + 2, 0, x] = ex[:1, :]
            send_y[2 * step + 2, 1, x] = ez[:1, :]
        else:
            set_plane(power, x, 0.5 * plane_of(sig, x) * added)

    loads[0].wait()

    def stage_e(x, _):
        send_y[0, 0, x] = e[0, x, :1, :]
        send_y[0, 1, x] = e[2, x, :1, :]
        return 0

    lax.fori_loop(0, cx, stage_e, 0)
    pl.semaphore_wait(barrier, n - 1)
    start_halo(0)
    loads[1].wait()
    lax.fori_loop(cuts[0], cuts[1], send_choice, 0)
    recv_c[me] = choice[maps[1, me]].astype(jnp.float32)
    loads[2].wait()
    loads[3].wait()

    def scales(x, _):
        four_eps, sigma = 4.0 * plane_of(eps, x), plane_of(sig, x)
        inverse = 1.0 / (four_eps + sigma)
        set_plane(scale_e, x, (four_eps - sigma) * inverse)
        set_plane(scale_c, x, 2.0 * inverse)
        return 0

    lax.fori_loop(0, cx, scales, 0)
    loads[4].wait()
    for step in range(STEPS):
        await_halo(2 * step)

        def h_body(x, _):
            h_plane(step, x, e[1, x + 1], e[2, x + 1])
            return 0

        lax.fori_loop(0, cx - 1, h_body, 0)
        h_plane(step, cx - 1, halo_x[2 * step, 0], halo_x[2 * step, 1])
        start_halo(2 * step + 1)
        lax.fori_loop(cuts[2 * step + 1], cuts[2 * step + 2], send_choice, 0)
        await_halo(2 * step + 1)

        def e_body(x, _):
            e_plane(step, x, h[1, x - 1], h[2, x - 1])
            return 0

        e_plane(step, 0, halo_x[2 * step + 1, 0], halo_x[2 * step + 1, 1])
        lax.fori_loop(1, cx, e_body, 0)
        if step < STEPS - 1:
            start_halo(2 * step + 2)
            lax.fori_loop(cuts[2 * step + 2], cuts[2 * step + 3], send_choice, 0)

    def send_power(d, _):
        t = lax.rem(me + d, n)
        send_p[t] = power[maps[0, t]]
        block_copy(send_p, recv_p, sp_sem, rp_sem, t, me).start()
        return 0

    lax.fori_loop(1, n, send_power, 0)
    field_stores = [
        pltpu.make_async_copy(e, e_out, out_sem.at[0]),
        pltpu.make_async_copy(h, h_out, out_sem.at[1]),
    ]
    for store in field_stores:
        store.start()
    recv_p[me] = power[maps[0, me]]
    loads[5].wait()
    loads[6].wait()
    block_lane = lax.broadcasted_iota(jnp.int32, (width, depth), 1)

    def thermal(s):
        slot = maps[1, s]
        state, water = temp[slot], wet[slot]
        above = jnp.where(block_lane == depth - 1, state, pltpu.roll(state, depth - 1, 1))
        below = jnp.where(block_lane == 0, state, pltpu.roll(state, 1, 1))
        warmed = (
            state
            + DIFFUSION_FACTOR * ((above - state) + (below - state))
            + WARMING_FACTOR * recv_p[s]
        )
        excess = jnp.maximum(warmed - BOILING, 0.0)
        vapour = water * (1.0 - jnp.exp(-EVAP_RATE * excess))
        tmp_m[s] = water - vapour
        tmp_t[s] = warmed - VAPOUR_ENTHALPY * vapour

    thermal(me)
    recv_m[me] = tmp_m[me]

    def thermal_body(d, _):
        s = lax.rem(me - d + n, n)
        block_copy(send_p, recv_p, sp_sem, rp_sem, s, s).wait_recv()
        thermal(s)
        block_copy(tmp_m, recv_m, sm_sem, rm_sem, s, me).start()
        return 0

    lax.fori_loop(1, n, thermal_body, 0)

    def order_blocks(k, _):
        s = maps[2, k]
        temp_stage[k] = tmp_t[s]
        moist_stage[k] = tmp_m[s]
        return 0

    lax.fori_loop(0, n, order_blocks, 0)
    block_stores = [
        pltpu.make_async_copy(temp_stage, temp_out, out_sem.at[2]),
        pltpu.make_async_copy(moist_stage, moist_out, out_sem.at[3]),
    ]
    for store in block_stores:
        store.start()

    levels = table.shape[1]

    def lookup(line, column):
        values = [table[column, q] for q in range(levels)]
        bit = 1
        while len(values) > 1:
            high = (line & bit) != 0
            values = [
                jnp.where(high, values[q + 1], values[q]) for q in range(0, len(values), 2)
            ]
            bit *= 2
        return values[0]

    def refresh(t):
        line = recv_c[t].astype(jnp.int32)
        water = recv_m[t]
        new_perm[t] = 1.0 + lookup(line, 0) + 4.0 * lookup(line, 1) * water
        new_cond[t] = 0.1 * lookup(line, 2) + 0.3 * lookup(line, 3) * water

    refresh(me)

    def refresh_body(d, _):
        t = lax.rem(me + d, n)
        block_copy(send_c, recv_c, sc_sem, rc_sem, t, t).wait_recv()
        block_copy(tmp_m, recv_m, sm_sem, rm_sem, t, t).wait_recv()
        refresh(t)
        return 0

    lax.fori_loop(1, n, refresh_body, 0)
    loads[7].wait()

    def settle(k, _):
        t = maps[3, k]
        product = lab[k] == 2
        perm_stage[k] = jnp.where(product, new_perm[t], eps[k])
        cond_stage[k] = jnp.where(product, new_cond[t], sig[k])
        return 0

    lax.fori_loop(0, n, settle, 0)
    cell_stores = [
        pltpu.make_async_copy(perm_stage, perm_out, out_sem.at[4]),
        pltpu.make_async_copy(cond_stage, cond_out, out_sem.at[5]),
    ]
    for store in cell_stores:
        store.start()

    def drain(d, _):
        t = lax.rem(me + d, n)
        block_copy(send_c, recv_c, sc_sem, rc_sem, t, me).wait_send()
        block_copy(send_p, recv_p, sp_sem, rp_sem, t, me).wait_send()
        block_copy(tmp_m, recv_m, sm_sem, rm_sem, t, me).wait_send()
        return 0

    lax.fori_loop(1, n, drain, 0)
    for store in field_stores + block_stores + cell_stores:
        store.wait()


def inverse_of(order):
    places = jnp.arange(order.shape[0], dtype=jnp.int32)
    return jnp.sum(jnp.where(order[None, :] == places[:, None], places[None, :], 0), axis=1)


def local(
    nx, ny,
    efield_vector,
    hfield_vector,
    dielectric_grid,
    sigma_grid,
    substance_label,
    thermal_state,
    wetness_share,
    dielectric_line_choice,
    dielectric_lookup_lines,
    dispatch_keeper_map,
    arrival_position_map,
):
    n = nx * ny
    _, cx, cy, depth = efield_vector.shape
    width = cx * cy // n
    keeper, arrival = dispatch_keeper_map[0], arrival_position_map[0]
    maps = jnp.stack([inverse_of(keeper), arrival, inverse_of(arrival), keeper])
    blocks = (n, width, depth)
    f32 = jnp.float32
    hbm = pl.BlockSpec(memory_space=pl.ANY)
    smem = pl.BlockSpec(memory_space=pltpu.SMEM)
    grid_f = pltpu.VMEM(blocks, f32)
    grid_i = pltpu.VMEM(blocks, jnp.int32)
    fields = pltpu.VMEM((3, cx, cy, depth), f32)
    dma = pltpu.SemaphoreType.DMA
    exchanges = 2 * STEPS
    shape_f = jax.ShapeDtypeStruct(efield_vector.shape, f32)
    shape_b = jax.ShapeDtypeStruct(blocks, f32)
    cells = cx * cy * depth
    efield, hfield, perm, cond, warmth, water = pl.pallas_call(
        functools.partial(kernel, nx, ny),
        out_shape=(shape_f, shape_f, shape_b, shape_b, shape_b, shape_b),
        in_specs=[smem, smem] + [hbm] * 8,
        out_specs=(hbm,) * 6,
        scratch_shapes=[
            fields, fields, grid_f, grid_f, grid_i, grid_f, grid_f, grid_i,
            grid_f, grid_f, grid_f, grid_f,
            grid_f, grid_f, grid_f, grid_f, grid_f, grid_f, grid_f,
            grid_f, grid_f, grid_f, grid_f, grid_f, grid_f,
            pltpu.VMEM((exchanges, 2, cx, 1, depth), f32),
            pltpu.VMEM((exchanges, 2, cy, depth), f32),
            pltpu.VMEM((exchanges, 2, cx, 1, depth), f32),
            dma((8,)), dma((6,)),
            dma((exchanges,)), dma((exchanges,)), dma((exchanges,)), dma((exchanges,)),
            dma((n,)), dma((n,)), dma((n,)), dma((n,)), dma((n,)), dma((n,)),
        ],
        compiler_params=pltpu.CompilerParams(
            collective_id=0, has_side_effects=True, vmem_limit_bytes=48 * 1024 * 1024
        ),
        cost_estimate=pl.CostEstimate(
            flops=200 * cells, bytes_accessed=22 * 4 * cells, transcendentals=cells
        ),
    )(
        maps, dielectric_lookup_lines, efield_vector, hfield_vector,
        dielectric_grid.reshape(blocks), sigma_grid.reshape(blocks),
        substance_label.reshape(blocks), thermal_state, wetness_share, dielectric_line_choice,
    )
    cavity = dielectric_grid.shape
    return efield, hfield, perm.reshape(cavity), cond.reshape(cavity), warmth, water


def solution(mesh):
    in_specs = (
        P(None, "gx", "gy", None),
        P(None, "gx", "gy", None),
        P("gx", "gy", None),
        P("gx", "gy", None),
        P("gx", "gy", None),
        P(("gx", "gy"), None, None),
        P(("gx", "gy"), None, None),
        P(("gx", "gy"), None, None),
        P(),
        P(("gx", "gy"), None),
        P(("gx", "gy"), None),
    )
    out_specs = (
        P(None, "gx", "gy", None),
        P(None, "gx", "gy", None),
        P("gx", "gy", None),
        P("gx", "gy", None),
        P(("gx", "gy"), None, None),
        P(("gx", "gy"), None, None),
    )
    body = functools.partial(local, mesh.shape["gx"], mesh.shape["gy"])
    return jax.shard_map(body, mesh=mesh, in_specs=in_specs, out_specs=out_specs, check_vma=False)
```

time: 169 us -> 98.9 us (0.59)
  Pallas kernels: 0 us -> 83.9 us
  waiting for transfers between devices: 55.6 us -> 0 us
  other arithmetic: 43.5 us -> 2.23 us
  starting transfers between devices: 36.7 us -> 0 us
  local copies, waits for them, and re-layouts: 30.8 us -> 11.6 us
    pallas_call x0 -> x1, Pallas kernels: none -> 83.9 us  [local(): pl.pallas_call(functools.partial(kernel, nx, ny), out_shape=(shape_f, sha...]
    all_to_all x3 -> x0, waiting for transfers between devices: 50.4 us -> none  [the longest x1 20.4 us: local(): lax.all_to_all(cond_rows, ('gx', 'gy'), split_axis=0, concat_axis=0, tile...]
    ppermute x8 -> x0, starting transfers between devices: 24.5 us -> none  [passed_along(): return lax.ppermute(value, axis, pairs)]
    gather x6 -> x0, local copies, waits for them, and re-layouts: 14.9 us -> none  [the longest x1 2.81 us: local(): wattage_each_tile = arrived[jnp.argsort(slots_here)]]
    all_to_all x3 -> x0, starting transfers between devices: 12.2 us -> none  [the longest x1 5.77 us: local(): lax.all_to_all(outgoing, ('gx', 'gy'), split_axis=0, concat_axis=0, tiled...]
    slice x28 -> x0, local copies, waits for them, and re-layouts: 12 us -> none  [the longest x11 7.32 us: forward_diff(): lax.slice_in_dim(values, 1, extent, axis=along)]
    sub x3 -> x0, other arithmetic: 11.9 us -> none  [the longest x1 5.23 us: local(): mag_y - TIME_STEP * (forward_diff(elec_x, zero_z, 2) - forward_diff(elec_...]
    unnamed x32 -> x12, local copies, waits for them, and re-layouts: 1.13 us -> 11.6 us
  transfers between devices with their start and end apart: 11 -> 0, of which waited for: 7 -> 0; matrix products, arithmetic and copies ran while one was open for 23% -> 0% of each run, Pallas kernels for 0% -> 0%
where the time goes in v1:
time: 98.9 us; the launch traced here: 98.4 us
  Pallas kernels  83.9 us (85%)
  local copies, waits for them, and re-layouts  11.6 us (12%)
  other arithmetic  2.23 us (2%)
    pallas_call x1, Pallas kernels, local(): pl.pallas_call(functools.partial(kernel, nx, ny), out_shape=(shape_f, sha...  83.9 us
    unnamed x12, local copies, waits for them, and re-layouts  11.6 us

profile of v1, /device:TPU:1, one launch (start us, length us, event | category | flops | bytes accessed | tf_op | source)
XLA Modules:
  0.0 98.4 jit_solution(6527774088793569565)
XLA Ops:
  0.6 0.8 select_reduce_fusion
  1.4 0.8 select_reduce_fusion.1
  2.2 0.7 pad_add_fusion.maps
  2.9 0.0 copy-start
  2.9 1.2 %copy-done = f32[32,32,256]{2,1,0:T(8,128)S(1)} copy-done((f32[32,32,256]{2,1,0:T(8,128)S(1)}, f32[32,32,256]{2,1,0:T(8,128)}, u32[]{:S(2)}) %copy-start) | copy-done | bytes 1048600
  4.1 0.0 copy-start.1
  4.1 0.7 copy-done.1
  4.8 83.9 %shard_map.154 = (f32[3,32,32,256]{3,2,1,0:T(8,128)}, f32[3,32,32,256]{3,2,1,0:T(8,128)}, f32[32,32,256]{2,1,0:T(8,128)S(1)}, f32[32,32,256]{2,1,0:T(8,128)S(1)}...) custom-call(s32[4,32]{1,0:T(4,128)S(1)} %pad_add_fusion.maps, f32[4,16]{1,0:T(4,128)S(1)} %copy-done.1, ...), custom_call_target="tpu_custom_call" | custom-call | flops 52428800 | bytes 23068672 | tf_op jit(solution)/shard_map/pallas_call | solution.py:379
  88.7 0.0 copy-start.2
  88.7 4.1 %copy.23 = f32[3,32,32,256]{3,2,1,0:T(8,128)} copy(f32[3,32,32,256]{3,2,1,0:T(8,128)} %get-tuple-element.12) | data formatting | bytes 6291456
  92.8 0.0 copy-done.2
  92.8 1.7 %copy.24 = f32[3,32,32,256]{3,2,1,0:T(8,128)} copy(f32[3,32,32,256]{3,2,1,0:T(8,128)S(1)} %copy-done.2) | data formatting | bytes 6291456
  94.5 1.0 copy.25
  95.4 1.0 copy.26
  96.4 1.0 copy.27
  97.4 1.0 copy.28
Async XLA Ops:
  2.9 1.2 %copy-start = (f32[32,32,256]{2,1,0:T(8,128)S(1)}, f32[32,32,256]{2,1,0:T(8,128)}, u32[]{:S(2)}) copy-start(f32[32,32,256]{2,1,0:T(8,128)} %eps_in.1) | copy-start | bytes 3145732
  4.1 0.7 copy-start.1
  88.7 4.1 %copy-start.2 = (f32[3,32,32,256]{3,2,1,0:T(8,128)S(1)}, f32[3,32,32,256]{3,2,1,0:T(8,128)}, u32[]{:S(2)}) copy-start(f32[3,32,32,256]{3,2,1,0:T(8,128)} %get-tuple-element.13) | copy-start | bytes 9437188

commit v2 on v1

--- a/solution.py
+++ b/solution.py
@@ -18,14 +18,14 @@
 
 
 def kernel(
-    nx, ny, maps, table,
+    nx, ny, keeper_in, arrival_in, table_in,
     e_in, h_in, eps_in, sig_in, lab_in, t_in, w_in, c_in,
     e_out, h_out, perm_out, cond_out, temp_out, moist_out,
     e, h, eps, sig, lab, temp, wet, choice,
     scale_e, scale_c, squares, power,
     send_c, recv_c, send_p, recv_p, tmp_t, tmp_m, recv_m,
     new_perm, new_cond, temp_stage, moist_stage, perm_stage, cond_stage,
-    send_y, halo_x, halo_y,
+    send_y, halo_x, halo_y, keeper, arrival, table, inverse_v, inverse,
     in_sem, out_sem, hx_send, hx_recv, hy_send, hy_recv,
     sc_sem, rc_sem, sp_sem, rp_sem, sm_sem, rm_sem,
 ):
@@ -40,6 +40,7 @@
     loads = [
         pltpu.make_async_copy(src, dst, in_sem.at[q])
         for q, (src, dst) in enumerate([
+            (arrival_in, arrival), (keeper_in, keeper), (table_in, table),
             (e_in, e), (c_in, choice), (eps_in, eps), (sig_in, sig), (h_in, h),
             (t_in, temp), (w_in, wet), (lab_in, lab),
         ])
@@ -120,7 +121,7 @@
 
     def send_choice(d, _):
         t = lax.rem(me + d, n)
-        send_c[t] = choice[maps[1, t]].astype(jnp.float32)
+        send_c[t] = choice[arrival[0, t]].astype(jnp.float32)
         block_copy(send_c, recv_c, sc_sem, rc_sem, t, me).start()
         return 0
 
@@ -175,7 +176,7 @@
         else:
             set_plane(power, x, 0.5 * plane_of(sig, x) * added)
 
-    loads[0].wait()
+    loads[3].wait()
 
     def stage_e(x, _):
         send_y[0, 0, x] = e[0, x, :1, :]
@@ -185,11 +186,23 @@
     lax.fori_loop(0, cx, stage_e, 0)
     pl.semaphore_wait(barrier, n - 1)
     start_halo(0)
+    loads[4].wait()
+    loads[0].wait()
     loads[1].wait()
     lax.fori_loop(cuts[0], cuts[1], send_choice, 0)
-    recv_c[me] = choice[maps[1, me]].astype(jnp.float32)
-    loads[2].wait()
-    loads[3].wait()
+    map_row = lax.broadcasted_iota(jnp.int32, inverse_v.shape, 0)
+    map_lane = lax.broadcasted_iota(jnp.int32, inverse_v.shape, 1)
+
+    def invert(k, places):
+        target = jnp.where(map_row == 0, keeper[0, k], arrival[0, k])
+        return jnp.where(map_lane == target, k, places)
+
+    inverse_v[...] = lax.fori_loop(0, n, invert, jnp.zeros(inverse_v.shape, jnp.int32))
+    invert_copy = pltpu.make_async_copy(inverse_v, inverse, in_sem.at[11])
+    invert_copy.start()
+    recv_c[me] = choice[arrival[0, me]].astype(jnp.float32)
+    loads[5].wait()
+    loads[6].wait()
 
     def scales(x, _):
         four_eps, sigma = 4.0 * plane_of(eps, x), plane_of(sig, x)
@@ -199,7 +212,7 @@
         return 0
 
     lax.fori_loop(0, cx, scales, 0)
-    loads[4].wait()
+    loads[7].wait()
     for step in range(STEPS):
         await_halo(2 * step)
 
@@ -223,9 +236,11 @@
             start_halo(2 * step + 2)
             lax.fori_loop(cuts[2 * step + 2], cuts[2 * step + 3], send_choice, 0)
 
+    invert_copy.wait()
+
     def send_power(d, _):
         t = lax.rem(me + d, n)
-        send_p[t] = power[maps[0, t]]
+        send_p[t] = power[inverse[0, t]]
         block_copy(send_p, recv_p, sp_sem, rp_sem, t, me).start()
         return 0
 
@@ -236,13 +251,13 @@
     ]
     for store in field_stores:
         store.start()
-    recv_p[me] = power[maps[0, me]]
-    loads[5].wait()
-    loads[6].wait()
+    recv_p[me] = power[inverse[0, me]]
+    loads[8].wait()
+    loads[9].wait()
     block_lane = lax.broadcasted_iota(jnp.int32, (width, depth), 1)
 
     def thermal(s):
-        slot = maps[1, s]
+        slot = arrival[0, s]
         state, water = temp[slot], wet[slot]
         above = jnp.where(block_lane == depth - 1, state, pltpu.roll(state, depth - 1, 1))
         below = jnp.where(block_lane == 0, state, pltpu.roll(state, 1, 1))
@@ -269,7 +284,7 @@
     lax.fori_loop(1, n, thermal_body, 0)
 
     def order_blocks(k, _):
-        s = maps[2, k]
+        s = inverse[1, k]
         temp_stage[k] = tmp_t[s]
         moist_stage[k] = tmp_m[s]
         return 0
@@ -282,6 +297,7 @@
     for store in block_stores:
         store.start()
 
+    loads[2].wait()
     levels = table.shape[1]
 
     def lookup(line, column):
@@ -311,10 +327,10 @@
         return 0
 
     lax.fori_loop(1, n, refresh_body, 0)
-    loads[7].wait()
+    loads[10].wait()
 
     def settle(k, _):
-        t = maps[3, k]
+        t = keeper[0, k]
         product = lab[k] == 2
         perm_stage[k] = jnp.where(product, new_perm[t], eps[k])
         cond_stage[k] = jnp.where(product, new_cond[t], sig[k])
@@ -340,9 +356,19 @@
         store.wait()
 
 
-def inverse_of(order):
-    places = jnp.arange(order.shape[0], dtype=jnp.int32)
-    return jnp.sum(jnp.where(order[None, :] == places[:, None], places[None, :], 0), axis=1)
+def hand_out(*refs):
+    sources, results, sem = refs[:6], refs[6:12], refs[12]
+    pairs = []
+    for source, result in zip(sources, results):
+        if len(source.shape) == 4:
+            pairs += [(source.at[q], result.at[q]) for q in range(3)]
+        else:
+            pairs.append((source, result))
+    copies = [pltpu.make_async_copy(a, b, sem.at[q]) for q, (a, b) in enumerate(pairs)]
+    for copy in copies:
+        copy.start()
+    for copy in copies:
+        copy.wait()
 
 
 def local(
@@ -362,12 +388,11 @@
     n = nx * ny
     _, cx, cy, depth = efield_vector.shape
     width = cx * cy // n
-    keeper, arrival = dispatch_keeper_map[0], arrival_position_map[0]
-    maps = jnp.stack([inverse_of(keeper), arrival, inverse_of(arrival), keeper])
     blocks = (n, width, depth)
     f32 = jnp.float32
     hbm = pl.BlockSpec(memory_space=pl.ANY)
-    smem = pl.BlockSpec(memory_space=pltpu.SMEM)
+    own = pl.BlockSpec(memory_space=pltpu.HBM)
+    lanes = max(128, n)
     grid_f = pltpu.VMEM(blocks, f32)
     grid_i = pltpu.VMEM(blocks, jnp.int32)
     fields = pltpu.VMEM((3, cx, cy, depth), f32)
@@ -376,10 +401,10 @@
     shape_f = jax.ShapeDtypeStruct(efield_vector.shape, f32)
     shape_b = jax.ShapeDtypeStruct(blocks, f32)
     cells = cx * cy * depth
-    efield, hfield, perm, cond, warmth, water = pl.pallas_call(
+    results = pl.pallas_call(
         functools.partial(kernel, nx, ny),
         out_shape=(shape_f, shape_f, shape_b, shape_b, shape_b, shape_b),
-        in_specs=[smem, smem] + [hbm] * 8,
+        in_specs=[own] * 11,
         out_specs=(hbm,) * 6,
         scratch_shapes=[
             fields, fields, grid_f, grid_f, grid_i, grid_f, grid_f, grid_i,
@@ -389,21 +414,32 @@
             pltpu.VMEM((exchanges, 2, cx, 1, depth), f32),
             pltpu.VMEM((exchanges, 2, cy, depth), f32),
             pltpu.VMEM((exchanges, 2, cx, 1, depth), f32),
-            dma((8,)), dma((6,)),
+            pltpu.SMEM((1, n), jnp.int32), pltpu.SMEM((1, n), jnp.int32),
+            pltpu.SMEM(dielectric_lookup_lines.shape, f32),
+            pltpu.VMEM((8, lanes), jnp.int32), pltpu.SMEM((8, lanes), jnp.int32),
+            dma((12,)), dma((6,)),
             dma((exchanges,)), dma((exchanges,)), dma((exchanges,)), dma((exchanges,)),
             dma((n,)), dma((n,)), dma((n,)), dma((n,)), dma((n,)), dma((n,)),
         ],
         compiler_params=pltpu.CompilerParams(
-            collective_id=0, has_side_effects=True, vmem_limit_bytes=48 * 1024 * 1024
+            collective_id=0, has_side_effects=True, vmem_limit_bytes=54 * 1024 * 1024
         ),
         cost_estimate=pl.CostEstimate(
             flops=200 * cells, bytes_accessed=22 * 4 * cells, transcendentals=cells
         ),
     )(
-        maps, dielectric_lookup_lines, efield_vector, hfield_vector,
+        dispatch_keeper_map, arrival_position_map, dielectric_lookup_lines, efield_vector, hfield_vector,
         dielectric_grid.reshape(blocks), sigma_grid.reshape(blocks),
         substance_label.reshape(blocks), thermal_state, wetness_share, dielectric_line_choice,
     )
+    efield, hfield, perm, cond, warmth, water = pl.pallas_call(
+        hand_out,
+        out_shape=(shape_f, shape_f, shape_b, shape_b, shape_b, shape_b),
+        in_specs=[hbm] * 6,
+        out_specs=(own,) * 6,
+        scratch_shapes=[dma((10,))],
+        compiler_params=pltpu.CompilerParams(vmem_limit_bytes=54 * 1024 * 1024),
+    )(*results)
     cavity = dielectric_grid.shape
     return efield, hfield, perm.reshape(cavity), cond.reshape(cavity), warmth, water
 

time: 98.9 us -> 404 us (4.08)
  Pallas kernels: 83.9 us -> 403 us
  local copies, waits for them, and re-layouts: 11.6 us -> 0 us
    pallas_call x0 -> x1, Pallas kernels: none -> 319 us  [local(): pl.pallas_call(hand_out, out_shape=(shape_f, shape_f, shape_b, shape_b, s...]
    unnamed x12 -> x0, local copies, waits for them, and re-layouts: 11.6 us -> none
where the time goes in v2:
time: 404 us
  Pallas kernels  403 us (100%)
    pallas_call x1, Pallas kernels, local(): pl.pallas_call(hand_out, out_shape=(shape_f, shape_f, shape_b, shape_b, s...  319 us
    pallas_call x1, Pallas kernels, local(): pl.pallas_call(functools.partial(kernel, nx, ny), out_shape=(shape_f, sha...  84.1 us

profile of v2, /device:TPU:1, one launch (start us, length us, event | category | flops | bytes accessed | tf_op | source)
XLA Modules:
  0.0 403.5 jit_solution(10267607941082465691)
XLA Ops:
  0.6 84.1 %shard_map.154 = (f32[3,32,32,256]{3,2,1,0:T(8,128)}, f32[3,32,32,256]{3,2,1,0:T(8,128)}, f32[32,32,256]{2,1,0:T(8,128)}, f32[32,32,256]{2,1,0:T(8,128)}, f32[32...) custom-call(s32[1,32]{1,0:T(1,128)} %keeper_in.1, s32[1,32]{1,0:T(1,128)} %arrival_in.1, f32[4,16]{1,0:T(4,128)} %table_in.1, ...), custom_call_target="tpu_custom_call" | custom-call | flops 52428800 | bytes 23068672 | tf_op jit(solution)/shard_map/pallas_call | solution.py:404
  84.7 318.8 %shard_map.155 = (f32[3,32,32,256]{3,2,1,0:T(8,128)}, f32[3,32,32,256]{3,2,1,0:T(8,128)}, f32[32,32,256]{2,1,0:T(8,128)}, f32[32,32,256]{2,1,0:T(8,128)}, f32[32...) custom-call(f32[3,32,32,256]{3,2,1,0:T(8,128)} %get-tuple-element.12.refs_0_, f32[3,32,32,256]{3,2,1,0:T(8,128)} %get-tuple-element.13.refs_1_, ...), custom_call_target="tpu_custom_call" | custom-call | tf_op jit(solution)/shard_map/pallas_call | solution.py:435
